TPU v7x, 128 devices: a whole 4x4x4 slice. The times are simulated.
128 devices in a mesh: dp: 8 (over z_lo, y), tensor: 16 (over x, z_hi, core).
Axes of the slice: x: 4, y: 4, z: 4 (z_hi: 2, z_lo: 2; z = z_hi * 2 + z_lo), core: 2. Of those that a mesh axis runs over, the one named last changes fastest.
Arguments:
- tokens: bfloat16 [8192, 8192], P('dp', 'tensor'), may hold values from -6 to 6
- up_first_weight: bfloat16 [64, 128, 512], P('tensor'), may hold values from -0.5 to 0.5
- up_left: bfloat16 [64, 512, 512], P('tensor'), may hold values from -0.25 to 0.25
- down_first_weight: bfloat16 [64, 512, 512], P('tensor'), may hold values from -0.25 to 0.25
- down_left: bfloat16 [64, 512, 128], P('tensor'), may hold values from -0.25 to 0.25
- out_grad: bfloat16 [8192, 8192], P('dp', 'tensor'), may hold values from -6 to 6
Outputs:
- layer_out: bfloat16 [8192, 8192], P('dp', 'tensor')
- input_grad: bfloat16 [8192, 8192], P('dp', 'tensor')
- grad_up_right: float32 [64, 128, 512], P('tensor', 'dp')
- grad_up_left: float32 [64, 512, 512], P('tensor', 'dp')
- grad_down_right: float32 [64, 512, 512], P('tensor', 'dp')
- grad_down_left: float32 [64, 512, 128], P('tensor', 'dp')
All inputs are finite; a program needn't handle non-finite values.
Results may differ from a plain program's by a relative error of at most 0.0064.
Values may be sent and summed in bfloat16 or wider, within the bound.
A program may use at most 128 MiB of HBM per device.

v0:
```python
import jax
import jax.numpy as jnp
from jax import lax
from jax.sharding import PartitionSpec as P


def per_device(tokens, up_first_weight, up_left, down_first_weight, down_left, out_grad):
    local_blocks = up_first_weight.shape[0]
    block_feat = up_first_weight.shape[1]
    block_hid = up_first_weight.shape[2]
    tensor_count = lax.axis_size("tensor")
    all_blocks = local_blocks * tensor_count
    sub_units = block_hid // all_blocks
    rows = tokens.shape[0]
    token_cube = tokens.reshape(rows, local_blocks, block_feat)
    grad_cube = out_grad.reshape(rows, local_blocks, block_feat)
    left_up = up_left.reshape(local_blocks, all_blocks, sub_units, block_hid)
    left_down = down_left.reshape(local_blocks, all_blocks, sub_units, block_feat)
    out_shape = (rows, local_blocks, tensor_count, local_blocks, sub_units)
    back_shape = (rows, tensor_count, local_blocks, local_blocks, sub_units)
    first_factor = jnp.einsum(
        "rlk,lkh->rlh", token_cube, up_first_weight, preferred_element_type=jnp.float32
    ).astype(jnp.bfloat16)
    mixed_up = lax.all_to_all(
        first_factor.reshape(out_shape), "tensor", split_axis=2, concat_axis=1, tiled=True
    )
    mixed_up = mixed_up.reshape(rows, all_blocks, local_blocks, sub_units)
    pre = jnp.einsum("rijt,jitn->rjn", mixed_up, left_up, preferred_element_type=jnp.float32)
    hidden_state = jax.nn.gelu(pre).astype(jnp.bfloat16)
    second_factor = jnp.einsum(
        "rln,lnm->rlm", hidden_state, down_first_weight, preferred_element_type=jnp.float32
    ).astype(jnp.bfloat16)
    mixed_down = lax.all_to_all(
        second_factor.reshape(out_shape), "tensor", split_axis=2, concat_axis=1, tiled=True
    )
    mixed_down = mixed_down.reshape(rows, all_blocks, local_blocks, sub_units)
    branch = jnp.einsum("rijt,jitn->rjn", mixed_down, left_down, preferred_element_type=jnp.float32)
    layer_out = (
        tokens.astype(jnp.float32) + branch.reshape(rows, local_blocks * block_feat)
    ).astype(jnp.bfloat16)
    grad_mixed_down = jnp.einsum(
        "rjn,jitn->rijt", grad_cube, left_down, preferred_element_type=jnp.float32
    ).astype(jnp.bfloat16)
    grad_dl = jnp.einsum(
        "rijt,rjn->jitn", mixed_down, grad_cube, preferred_element_type=jnp.float32
    ).reshape(local_blocks, block_hid, block_feat)
    second_grad = lax.all_to_all(
        grad_mixed_down.reshape(back_shape), "tensor", split_axis=1, concat_axis=3, tiled=True
    )
    second_grad = second_grad.reshape(rows, local_blocks, block_hid)
    grad_dr = jnp.einsum(
        "rln,rlm->lnm", hidden_state, second_grad, preferred_element_type=jnp.float32
    )
    hidden_gradient = jnp.einsum(
        "rlm,lnm->rln", second_grad, down_first_weight, preferred_element_type=jnp.float32
    )
    grad_pre = jax.vjp(jax.nn.gelu, pre)[1](hidden_gradient)[0].astype(jnp.bfloat16)
    grad_ul = jnp.einsum(
        "rijt,rjn->jitn", mixed_up, grad_pre, preferred_element_type=jnp.float32
    ).reshape(local_blocks, block_hid, block_hid)
    grad_mixed_up = jnp.einsum(
        "rjn,jitn->rijt", grad_pre, left_up, preferred_element_type=jnp.float32
    ).astype(jnp.bfloat16)
    first_grad = lax.all_to_all(
        grad_mixed_up.reshape(back_shape), "tensor", split_axis=1, concat_axis=3, tiled=True
    )
    first_grad = first_grad.reshape(rows, local_blocks, block_hid)
    grad_ur = jnp.einsum("rlk,rlh->lkh", token_cube, first_grad, preferred_element_type=jnp.float32)
    sum_ur, sum_ul, sum_dr, sum_dl = (
        lax.psum_scatter(grad_ur, "dp", scatter_dimension=1, tiled=True),
        lax.psum_scatter(grad_ul, "dp", scatter_dimension=1, tiled=True),
        lax.psum_scatter(grad_dr, "dp", scatter_dimension=1, tiled=True),
        lax.psum_scatter(grad_dl, "dp", scatter_dimension=1, tiled=True),
    )
    backward_pass = jnp.einsum(
        "rlh,lkh->rlk", first_grad, up_first_weight, preferred_element_type=jnp.float32
    )
    input_grad = (
        out_grad.astype(jnp.float32) + backward_pass.reshape(rows, local_blocks * block_feat)
    ).astype(jnp.bfloat16)
    return (layer_out, input_grad, sum_ur, sum_ul, sum_dr, sum_dl)


def solution(mesh):
    return jax.shard_map(
        per_device,
        mesh=mesh,
        in_specs=(
            P("dp", "tensor"),
            P("tensor", None, None),
            P("tensor", None, None),
            P("tensor", None, None),
            P("tensor", None, None),
            P("dp", "tensor"),
        ),
        out_specs=(
            P("dp", "tensor"),
            P("dp", "tensor"),
            P("tensor", "dp", None),
            P("tensor", "dp", None),
            P("tensor", "dp", None),
            P("tensor", "dp", None),
        ),
        check_vma=False,
    )
```

profile of v0, /device:TPU:1, one launch (start us, length us, event | category | flops | bytes accessed | tf_op | source)
XLA Modules:
  0.0 492.7 jit_solution(2370703518749522763)
XLA Ops:
  7.2 0.0 copy-start
  7.2 2.8 convolution_convert_fusion.2
  10.0 2.4 copy.82
  12.4 9.1 %all-to-all-start = ((bf16[1024,4,16,4,8]{0,4,3,1,2:T(8,128)(2,1)}), bf16[1024,4,16,4,8]{0,4,3,1,2:T(8,128)(2,1)}, u32[]{:S(2)}, u32[]{:S(2)}) async-start(bf16[1024,4,16,4,8]{0,4,3,1,2:T(8,128)(2,1)} %copy.82), calls=%async_computation | async-start | bytes 8388608 | tf_op jit(solution)/shard_map/all_to_all | solution.py:24
  21.5 1.3 reshape.72
  22.9 2.3 convolution_convert_fusion.1
  25.2 2.4 copy.91
  27.6 46.7 %all-to-all-done = bf16[1024,4,16,4,8]{0,4,3,1,2:T(8,128)(2,1)} async-done(((bf16[1024,4,16,4,8]{0,4,3,1,2:T(8,128)(2,1)}), bf16[1024,4,16,4,8]{0,4,3,1,2:T(8,128)(2,1)}, u32[]{:S(2)}, u32[]{:S(2)}) %all-to-all-start) | async-done | bytes 4194336 | tf_op jit(solution)/shard_map/all_to_all | solution.py:24
  74.2 13.4 %all-to-all-start.2 = ((bf16[1024,16,4,4,8]{0,4,3,2,1:T(8,128)(2,1)}), bf16[1024,16,4,4,8]{0,4,3,2,1:T(8,128)(2,1)}, u32[]{:S(2)}, u32[]{:S(2)}) async-start(bf16[1024,16,4,4,8]{0,4,3,2,1:T(8,128)(2,1)} %copy.91), calls=%async_computation.2 | async-start | bytes 8388608 | tf_op jit(solution)/shard_map/all_to_all | solution.py:47
  87.7 0.0 copy-done
  87.7 9.9 %fusion.16 = f32[4,1024,512,1]{2,1,3,0:T(8,128)} fusion(bf16[1024,64,4,8]{0,3,2,1:T(8,128)(2,1)} %bitcast.4, bf16[4,64,8,512]{3,2,1,0:T(8,128)(2,1)S(1)} %bitcast.117), kind=kOutput, calls=%fused_computation.21 | convolution fusion | flops 2147483648 | bytes 14680064 | tf_op jit(solution)/shard_map/rijt,jitn->rjn/dot_general | solution.py:28
  97.6 42.7 %all-to-all-done.2 = bf16[1024,16,4,4,8]{0,4,3,2,1:T(8,128)(2,1)} async-done(((bf16[1024,16,4,4,8]{0,4,3,2,1:T(8,128)(2,1)}), bf16[1024,16,4,4,8]{0,4,3,2,1:T(8,128)(2,1)}, u32[]{:S(2)}, u32[]{:S(2)}) %all-to-all-start.2) | async-done | bytes 4194336 | tf_op jit(solution)/shard_map/all_to_all | solution.py:47
  140.3 0.0 copy-start.8
  140.3 2.8 copy.92
  143.1 0.0 copy-start.3
  143.1 1.9 copy-done.3
  145.1 0.0 copy-done.8
  145.1 10.2 %fusion.6 = bf16[1024,4,512]{2,0,1:T(8,128)(2,1)S(1)} fusion(f32[4,1024,512,1]{2,1,3,0:T(8,128)} %fusion.16, bf16[1024,4,512]{0,2,1:T(8,128)(2,1)S(1)} %bitcast.127, bf16[4,512,512]{2,1,0:T(8,128)(2,1)S(1)} %copy-done.8), kind=kOutput, calls=%fused_computation.8 | convolution fusion | flops 2189426688 | bytes 18874368 | tf_op jit(solution)/shard_map/rlm,lnm->rln/dot_general | solution.py:54
  155.3 0.0 copy-start.11
  155.3 2.4 convert_bitcast_fusion
  157.7 0.0 copy-done.11
  157.7 4.3 copy.122
  162.0 13.0 %all-to-all-start.3 = ((bf16[1024,16,4,4,8]{0,4,3,2,1:T(8,128)(2,1)}), bf16[1024,16,4,4,8]{0,4,3,2,1:T(8,128)(2,1)}, u32[]{:S(2)}, u32[]{:S(2)}) async-start(bf16[1024,16,4,4,8]{0,4,3,2,1:T(8,128)(2,1)} %bitcast.122), calls=%async_computation.3 | async-start | bytes 8388608 | tf_op jit(solution)/shard_map/all_to_all | solution.py:64
  175.0 0.0 copy-done.9
  175.0 7.0 %convolution_convert_fusion = bf16[4,1024,512]{1,2,0:T(8,128)(2,1)S(1)} fusion(bf16[4,512,512]{2,1,0:T(8,128)(2,1)S(1)} %copy-done.9, f32[4,1024,512,1]{2,1,3,0:T(8,128)} %fusion.16), kind=kOutput, calls=%fused_computation.28 | convolution fusion | flops 2168455168 | bytes 14680064 | tf_op jit(solution)/shard_map/rln,lnm->rlm/dot_general | solution.py:30
  182.0 2.8 copy.86
  184.7 43.0 %all-to-all-done.3 = bf16[1024,16,4,4,8]{0,4,3,2,1:T(8,128)(2,1)} async-done(((bf16[1024,16,4,4,8]{0,4,3,2,1:T(8,128)(2,1)}), bf16[1024,16,4,4,8]{0,4,3,2,1:T(8,128)(2,1)}, u32[]{:S(2)}, u32[]{:S(2)}) %all-to-all-start.3) | async-done | bytes 4194336 | tf_op jit(solution)/shard_map/all_to_all | solution.py:64
  227.7 13.0 %all-to-all-start.1 = ((bf16[1024,4,16,4,8]{0,4,3,1,2:T(8,128)(2,1)}), bf16[1024,4,16,4,8]{0,4,3,1,2:T(8,128)(2,1)}, u32[]{:S(2)}, u32[]{:S(2)}) async-start(bf16[1024,4,16,4,8]{0,4,3,1,2:T(8,128)(2,1)} %copy.86), calls=%async_computation.1 | async-start | bytes 8388608 | tf_op jit(solution)/shard_map/all_to_all | solution.py:33
  240.7 0.0 all-reduce.3.cloned.1.call-start
  240.7 2.7 copy.96
  243.4 0.0 copy-start.2
  243.4 2.0 copy-done.2
  245.4 0.0 copy-done.5
  245.4 1.2 convolution_bitcast_fusion
  246.7 1.4 copy.100
  248.1 0.0 all-reduce.3.cloned.1.call-update
  248.1 0.2 reduce-scatter.8.cloned.1.call-start
  248.3 53.5 %all-to-all-done.1 = bf16[1024,4,16,4,8]{0,4,3,1,2:T(8,128)(2,1)} async-done(((bf16[1024,4,16,4,8]{0,4,3,1,2:T(8,128)(2,1)}), bf16[1024,4,16,4,8]{0,4,3,1,2:T(8,128)(2,1)}, u32[]{:S(2)}, u32[]{:S(2)}) %all-to-all-start.1) | async-done | bytes 4194336 | tf_op jit(solution)/shard_map/all_to_all | solution.py:33
  301.8 6.7 %fusion.18 = f32[4,64,8,128]{3,1,2,0:T(8,128)S(1)} fusion(bf16[1024,64,4,8]{0,3,2,1:T(8,128)(2,1)} %bitcast.14, bf16[1024,4,128,1]{2,1,0,3:T(4,128)(2,1)S(1)} %bitcast.126), kind=kOutput, calls=%fused_computation.24 | convolution fusion | flops 536870912 | bytes 6291456 | tf_op jit(solution)/shard_map/rijt,rjn->jitn/dot_general | solution.py:44
  308.6 1.6 copy.156
  310.2 0.0 reduce-scatter.8.cloned.1.call-update
  310.2 0.0 reduce-scatter.4.cloned.1.call-start
  310.2 7.8 %fusion.24 = f32[4,512,512]{2,1,0:T(8,128)} fusion(bf16[1024,4,512]{2,0,1:T(8,128)(2,1)} %copy-done.11, bf16[1024,64,4,8]{0,3,2,1:T(8,128)(2,1)} %bitcast.4), kind=kOutput, calls=%fused_computation.31 | convolution fusion | flops 2147483648 | bytes 12582912 | tf_op jit(solution)/shard_map/rijt,rjn->jitn/dot_general | solution.py:58
  318.0 0.0 reduce-scatter.4.cloned.1.call-update
  318.0 0.3 reduce-scatter.6.cloned.1.call-start
  318.3 10.9 %fusion.39 = f32[4,512,512]{2,1,0:T(8,128)} fusion(bf16[1024,4,512]{0,2,1:T(8,128)(2,1)} %bitcast.128, f32[4,1024,512,1]{2,1,3,0:T(8,128)} %fusion.16), kind=kOutput, calls=%fused_computation.47 | convolution fusion | flops 2166358016 | bytes 16777216 | tf_op jit(solution)/shard_map/rln,rlm->lnm/dot_general | solution.py:51
  329.3 0.0 reduce-scatter.6.cloned.1.call-update
  329.3 0.6 copy-done.10
  329.9 0.6 dynamic-slice
  331.1 0.0 copy-done.7
  331.2 0.0 copy-start.6
  331.2 8.4 %fusion.20 = f32[4,1024,128,1]{1,2,3,0:T(8,128)} fusion(bf16[1024,64,4,8]{0,3,2,1:T(8,128)(2,1)} %bitcast.14, bf16[4,64,8,128]{3,2,1,0:T(8,128)(2,1)S(1)} %bitcast.132), kind=kOutput, calls=%fused_computation.26 | convolution fusion | flops 536870912 | bytes 6815744 | tf_op jit(solution)/shard_map/rijt,jitn->rjn/dot_general | solution.py:37
  339.6 2.9 copy.89
  342.4 0.0 copy-done.6
  342.4 4.2 fusion.42
  346.7 3.0 copy.98
  349.7 0.0 copy-done.4
  349.7 4.5 add_convert_fusion
  354.3 0.9 constant_dynamic-slice_fusion
  355.2 0.7 copy.106
  355.9 15.5 %reduce-scatter.8.cloned.1.call-done = f32[4,64,128]{2,1,0:T(8,128)} async-done(((f32[4,512,128]{2,1,0:T(8,128)}), f32[4,64,128]{2,1,0:T(8,128)}) %reduce-scatter.8.cloned.1.call-update) | async-done | bytes 131088 | tf_op jit(solution)/shard_map/reduce_scatter | solution.py:73
  371.4 59.7 %reduce-scatter.4.cloned.1.call-done = f32[4,64,512]{2,1,0:T(8,128)} async-done(((f32[4,512,512]{2,1,0:T(8,128)}), f32[4,64,512]{2,1,0:T(8,128)}) %reduce-scatter.4.cloned.1.call-update) | async-done | bytes 524304 | tf_op jit(solution)/shard_map/reduce_scatter | solution.py:71
  431.1 54.8 %reduce-scatter.6.cloned.1.call-done = f32[4,64,512]{2,1,0:T(8,128)} async-done(((f32[4,512,512]{2,1,0:T(8,128)}), f32[4,64,512]{2,1,0:T(8,128)}) %reduce-scatter.6.cloned.1.call-update) | async-done | bytes 524304 | tf_op jit(solution)/shard_map/reduce_scatter | solution.py:72
  485.9 0.0 copy-done.1
  (7 shorter events, 0.0 us)
Async XLA Ops:
  7.2 80.5 %copy-start = (bf16[4,512,512]{2,1,0:T(8,128)(2,1)S(1)}, bf16[4,512,512]{2,1,0:T(8,128)(2,1)}, u32[]{:S(2)}) copy-start(bf16[4,512,512]{2,1,0:T(8,128)(2,1)} %param.8) | copy-start | bytes 6291460
  12.4 61.8 %all-to-all-start = ((bf16[1024,4,16,4,8]{0,4,3,1,2:T(8,128)(2,1)}), bf16[1024,4,16,4,8]{0,4,3,1,2:T(8,128)(2,1)}, u32[]{:S(2)}, u32[]{:S(2)}) async-start(bf16[1024,4,16,4,8]{0,4,3,1,2:T(8,128)(2,1)} %copy.82), calls=%async_computation | async-start | bytes 8388608 | tf_op jit(solution)/shard_map/all_to_all | solution.py:24
  74.2 66.0 %all-to-all-start.2 = ((bf16[1024,16,4,4,8]{0,4,3,2,1:T(8,128)(2,1)}), bf16[1024,16,4,4,8]{0,4,3,2,1:T(8,128)(2,1)}, u32[]{:S(2)}, u32[]{:S(2)}) async-start(bf16[1024,16,4,4,8]{0,4,3,2,1:T(8,128)(2,1)} %copy.91), calls=%async_computation.2 | async-start | bytes 8388608 | tf_op jit(solution)/shard_map/all_to_all | solution.py:47
  140.3 4.8 copy-start.8
  143.1 1.9 copy-start.3
  155.3 2.4 copy-start.11
  162.0 13.0 %copy-start.9 = (bf16[4,512,512]{2,1,0:T(8,128)(2,1)S(1)}, bf16[4,512,512]{2,1,0:T(8,128)(2,1)}, u32[]{:S(2)}) copy-start(bf16[4,512,512]{2,1,0:T(8,128)(2,1)} %param.9) | copy-start | bytes 6291460
  162.0 65.7 %all-to-all-start.3 = ((bf16[1024,16,4,4,8]{0,4,3,2,1:T(8,128)(2,1)}), bf16[1024,16,4,4,8]{0,4,3,2,1:T(8,128)(2,1)}, u32[]{:S(2)}, u32[]{:S(2)}) async-start(bf16[1024,16,4,4,8]{0,4,3,2,1:T(8,128)(2,1)} %bitcast.122), calls=%async_computation.3 | async-start | bytes 8388608 | tf_op jit(solution)/shard_map/all_to_all | solution.py:64
  227.7 74.1 %all-to-all-start.1 = ((bf16[1024,4,16,4,8]{0,4,3,1,2:T(8,128)(2,1)}), bf16[1024,4,16,4,8]{0,4,3,1,2:T(8,128)(2,1)}, u32[]{:S(2)}, u32[]{:S(2)}) async-start(bf16[1024,4,16,4,8]{0,4,3,1,2:T(8,128)(2,1)} %copy.86), calls=%async_computation.1 | async-start | bytes 8388608 | tf_op jit(solution)/shard_map/all_to_all | solution.py:33
  240.7 4.8 copy-start.5
  240.7 113.6 %all-reduce.3.cloned.1.call-start = ((), (), s32[]{:S(2)}) async-start(), calls=%async_computation.10 | async-start | bytes 2097152
  243.4 2.0 copy-start.2
  248.1 123.3 %reduce-scatter.8.cloned.1.call-start = ((), (), s32[]{:S(2)}) async-start(), calls=%async_computation.9 | async-start | bytes 1179648 | tf_op jit(solution)/shard_map/reduce_scatter | solution.py:73
  310.2 120.9 %reduce-scatter.4.cloned.1.call-start = ((), (), s32[]{:S(2)}) async-start(), calls=%async_computation.7 | async-start | bytes 4718592 | tf_op jit(solution)/shard_map/reduce_scatter | solution.py:71
  318.0 167.9 %reduce-scatter.6.cloned.1.call-start = ((), (), s32[]{:S(2)}) async-start(), calls=%async_computation.8 | async-start | bytes 4718592 | tf_op jit(solution)/shard_map/reduce_scatter | solution.py:72
  329.3 0.7 copy-start.10
  329.3 1.9 copy-start.7
  331.2 11.3 %copy-start.6 = (bf16[4,128,512]{2,1,0:T(8,128)(2,1)S(1)}, bf16[4,128,512]{2,1,0:T(8,128)(2,1)}, u32[]{:S(2)}) copy-start(bf16[4,128,512]{2,1,0:T(8,128)(2,1)} %param.7) | copy-start | bytes 1572868
  346.7 3.1 copy-start.4
  346.7 139.2 %copy-start.1 = (bf16[4,512,512]{2,1,0:T(8,128)(2,1)S(1)}, bf16[4,512,512]{2,1,0:T(8,128)(2,1)}, u32[]{:S(2)}) copy-start(bf16[4,512,512]{2,1,0:T(8,128)(2,1)} %param.8) | copy-start | bytes 6291460
Sparse Core Ops, SparseCore 0:
  248.2 81.2 all-reduce.2
  332.5 38.9 reduce-scatter.7
  374.4 56.6 reduce-scatter.3
  434.0 51.8 reduce-scatter.5
where the time goes:
time: 497 us; the launch traced here: 493 us
  waiting for transfers between devices  316 us (64%)
  matrix products  73.9 us (15%)
  starting transfers between devices  49 us (10%)
  local copies, waits for them, and re-layouts  34.4 us (7%)
  between operations  14.8 us (3%)
    reduce_scatter x1, waiting for transfers between devices, per_device(): lax.psum_scatter(grad_ul, 'dp', scatter_dimension=1, tiled=True)  59.7 us
    reduce_scatter x1, waiting for transfers between devices, per_device(): lax.psum_scatter(grad_dr, 'dp', scatter_dimension=1, tiled=True)  54.8 us
    all_to_all x1, waiting for transfers between devices, per_device(): lax.all_to_all(second_factor.reshape(out_shape), 'tensor', split_axis=2,...  53.5 us
    all_to_all x1, waiting for transfers between devices, per_device(): lax.all_to_all(first_factor.reshape(out_shape), 'tensor', split_axis=2, c...  46.7 us
    all_to_all x1, waiting for transfers between devices, per_device(): lax.all_to_all(grad_mixed_up.reshape(back_shape), 'tensor', split_axis=1,...  43 us
    all_to_all x1, waiting for transfers between devices, per_device(): lax.all_to_all(grad_mixed_down.reshape(back_shape), 'tensor', split_axis=...  42.7 us
    reduce_scatter x1, waiting for transfers between devices, per_device(): lax.psum_scatter(grad_dl, 'dp', scatter_dimension=1, tiled=True)  15.5 us
    all_to_all x1, starting transfers between devices, per_device(): lax.all_to_all(grad_mixed_down.reshape(back_shape), 'tensor', split_axis=...  13.4 us
  transfers between devices with their start and end apart: 8, of which 7 were waited for; matrix products, arithmetic and copies ran while one was open for 17% of the time, Pallas kernels for 0%

commit v1 on v0

v1 whole, which is shorter than its diff:
```python
import functools

import jax
import jax.numpy as jnp
from jax import lax
from jax.experimental import pallas as pl
from jax.experimental.pallas import tpu as pltpu
from jax.sharding import PartitionSpec as P

NC = 4
R = 256
ND = 16
NB = 4
H = 512
D = 128
BF = jnp.bfloat16
F32 = jnp.float32


def mm(a, b):
    return lax.dot_general(a, b, (((1,), (0,)), ((), ())), preferred_element_type=F32)


def mm_nt(a, b):
    return lax.dot_general(a, b, (((1,), (1,)), ((), ())), preferred_element_type=F32)


def kernel(
    tok, w1, ul, df, dl, og,
    lo, ig, gur_o, gul_o, gdr_o, gdl_o,
    w1t, ult, dft, dlt, tokt,
    recv_a, recv_b, recv_c, recv_d, send_a, send_c, hid, dgel,
    gdls, gurs, r1_ul, r1_dr, r1_dl, r_ur,
    p2s_ul, p2s_dr, p2s_dl, p2r_ul, p2r_dr, p2r_dl,
    ssem, rsem, s1, q1, s2, q2, sur, qur,
):
    me = lax.axis_index("tensor")
    dp = lax.axis_index("dp")
    y = lax.rem(dp, 4)
    zl = dp // 4
    zo = 1 - zl

    barrier = pltpu.get_barrier_semaphore()

    def greet_t(k, _):
        pl.semaphore_signal(barrier, inc=1, device_id={"tensor": lax.rem(me + k, ND)}, device_id_type=pl.DeviceIdType.MESH)
        return 0

    def greet_d(k, _):
        pl.semaphore_signal(barrier, inc=1, device_id={"dp": lax.rem(dp + k, 8)}, device_id_type=pl.DeviceIdType.MESH)
        return 0

    lax.fori_loop(1, ND, greet_t, 0)
    lax.fori_loop(1, 8, greet_d, 0)

    for l in range(NB):
        w1t[l] = w1[l].T
    pl.semaphore_wait(barrier, ND - 1 + 7)

    def send(ph, c, sbuf, rbuf):
        def one(k, _):
            p = lax.rem(me + k, ND)
            pltpu.make_async_remote_copy(
                src_ref=sbuf.at[c, p], dst_ref=rbuf.at[c, me],
                send_sem=ssem.at[ph, c], recv_sem=rsem.at[ph, c],
                device_id={"tensor": p}, device_id_type=pl.DeviceIdType.MESH,
            ).start()
            return 0

        pltpu.make_async_copy(sbuf.at[c, me], rbuf.at[c, me], rsem.at[ph, c]).start()
        lax.fori_loop(1, ND, one, 0)

    def wait_recv(ph, c, rbuf):
        pltpu.make_async_copy(rbuf.at[c], rbuf.at[c], rsem.at[ph, c]).wait()

    def wait_send(ph, c, sbuf):
        view = sbuf.at[c, pl.ds(0, ND - 1)]
        pltpu.make_async_copy(view, view, ssem.at[ph, c]).wait()

    def rows(c):
        return pl.ds(pl.multiple_of(c * R, R), R)

    def pack(parts, axis, shape):
        return jnp.concatenate([p.reshape(shape) for p in parts], axis=axis).reshape(8, NB, 32, R).astype(BF)

    def first_stage(c, _):
        tokt[c] = tok[rows(c), :].T
        for g in range(2):
            parts = [mm(w1t[l, 256 * g:256 * g + 256, :], tokt[c, D * l:D * l + D, :]) for l in range(NB)]
            send_a[c, 8 * g:8 * g + 8] = pack(parts, 1, (32, 1, 8, R))
        send(0, c, send_a, recv_a)
        return 0

    def gmd_stage(c, _):
        for g in range(2):
            parts = [mm_nt(dl[j, 256 * g:256 * g + 256, :], og[rows(c), D * j:D * j + D]) for j in range(NB)]
            send_c[c, 8 * g:8 * g + 8] = pack(parts, 2, (8, 4, 1, 8, R))
        send(2, c, send_c, recv_c)
        return 0

    def mid_stage(c, _):
        wait_recv(0, c, recv_a)
        wait_send(0, c, send_a)

        def act(j, _):
            x = mm(ult[j].reshape(H, H), recv_a[c, :, j].reshape(H, R))
            x2 = x * x
            k0 = 0.7978845608028654
            t = jnp.tanh(k0 * x * (1.0 + 0.044715 * x2))
            half = 0.5 * (1.0 + t)
            hid[c, j] = (x * half).astype(BF)
            dgel[c, j] = (half + (0.5 * k0) * x * (1.0 - t * t) * (1.0 + (3 * 0.044715) * x2)).astype(BF)
            return 0

        lax.fori_loop(0, NB, act, 0)
        for g in range(2):
            parts = [mm(dft[l, g].reshape(256, H), hid[c, l]) for l in range(NB)]
            send_a[c, 8 * g:8 * g + 8] = pack(parts, 1, (32, 1, 8, R))
        send(1, c, send_a, recv_b)
        return 0

    def back_stage(c, _):
        wait_recv(2, c, recv_c)
        wait_send(2, c, send_c)

        def act(l, _):
            hg = mm(df[l], recv_c[c, :, l].reshape(H, R))
            dgel[c, l] = (hg * dgel[c, l].astype(F32)).astype(BF)
            return 0

        lax.fori_loop(0, NB, act, 0)
        for g in range(2):
            parts = [mm(ul[j, 256 * g:256 * g + 256, :], dgel[c, j]) for j in range(NB)]
            send_c[c, 8 * g:8 * g + 8] = pack(parts, 2, (8, 4, 1, 8, R))
        send(3, c, send_c, recv_d)
        return 0

    def out_stage(c, _):
        wait_recv(1, c, recv_b)
        for j in range(NB):
            b = mm(dlt[j], recv_b[c, :, j].reshape(H, R))
            lo[rows(c), D * j:D * j + D] = (tok[rows(c), D * j:D * j + D].astype(F32) + b.T).astype(BF)
        return 0

    def in_stage(c, _):
        for l in range(NB):
            b = mm(w1[l], recv_d[c, :, l].reshape(H, R))
            ig[rows(c), D * l:D * l + D] = (og[rows(c), D * l:D * l + D].astype(F32) + b.T).astype(BF)
        return 0

    def scatter_y(i, gs, r1):
        for k in range(1, 4):
            yp = lax.rem(y + k, 4)
            pltpu.make_async_remote_copy(
                src_ref=gs.at[:, :, yp], dst_ref=r1.at[k - 1],
                send_sem=s1.at[i, k - 1], recv_sem=q1.at[i, k - 1],
                device_id={"dp": zl * 4 + yp}, device_id_type=pl.DeviceIdType.MESH,
            ).start()

    def add_y(i, gs, r1, p2s, p2r, out):
        for k in range(1, 4):
            pltpu.make_async_copy(r1.at[k - 1], r1.at[k - 1], q1.at[i, k - 1]).wait()

        def total(l, z):
            t = gs[l, z, y].astype(F32)
            for k in range(3):
                t = t + r1[k, l, z].astype(F32)
            return t

        def to_send(l, _):
            p2s[l] = total(l, zo).astype(BF)
            return 0

        lax.fori_loop(0, NB, to_send, 0)
        pltpu.make_async_remote_copy(
            src_ref=p2s, dst_ref=p2r, send_sem=s2.at[i], recv_sem=q2.at[i],
            device_id={"dp": zo * 4 + y}, device_id_type=pl.DeviceIdType.MESH,
        ).start()

        def to_keep(l, _):
            out[l] = total(l, zl)
            return 0

        lax.fori_loop(0, NB, to_keep, 0)

    def add_z(i, gs, r1, p2s, p2r, out):
        pltpu.make_async_copy(p2r, p2r, q2.at[i]).wait()
        out[...] += p2r[...].astype(F32)
        pltpu.make_async_copy(p2s, p2s, s2.at[i]).wait()
        for k in range(1, 4):
            pltpu.make_async_copy(r1.at[k - 1], r1.at[k - 1], s1.at[i, k - 1]).wait()

    lax.fori_loop(0, NC, first_stage, 0)
    lax.fori_loop(0, NC, gmd_stage, 0)

    def prep(l, _):
        u = ul[l].T
        ult[l, 0] = u[0:256].reshape(4, 64, H)
        ult[l, 1] = u[256:512].reshape(4, 64, H)
        v = df[l].T
        dft[l, 0] = v[0:256].reshape(4, 64, H)
        dft[l, 1] = v[256:512].reshape(4, 64, H)
        dlt[l] = dl[l].T
        return 0

    lax.fori_loop(0, NB, prep, 0)
    lax.fori_loop(0, NC, mid_stage, 0)
    lax.fori_loop(0, NC, back_stage, 0)

    def grad_right(l, _):
        for g in range(2):
            acc = None
            for c in range(NC):
                v = mm_nt(hid[c, l, 256 * g:256 * g + 256, :], recv_c[c, :, l].reshape(H, R))
                acc = v if acc is None else acc + v
            dft[l, g] = acc.reshape(4, 64, H).astype(BF)
        return 0

    lax.fori_loop(0, NB, grad_right, 0)
    dr = (0, dft, r1_dr, p2s_dr, p2r_dr, gdr_o)
    scatter_y(*dr[:3])

    def grad_left(j, _):
        for g in range(2):
            acc = None
            for c in range(NC):
                v = mm_nt(recv_a[c, 8 * g:8 * g + 8, j].reshape(256, R), dgel[c, j])
                acc = v if acc is None else acc + v
            ult[j, g] = acc.reshape(4, 64, H).astype(BF)
        return 0

    lax.fori_loop(0, NB, grad_left, 0)
    ulx = (1, ult, r1_ul, p2s_ul, p2r_ul, gul_o)
    scatter_y(*ulx[:3])

    lax.fori_loop(0, NC, out_stage, 0)

    for j in range(NB):
        for g in range(2):
            acc = None
            for c in range(NC):
                v = mm(recv_b[c, 8 * g:8 * g + 8, j].reshape(256, R), og[R * c:R * c + R, D * j:D * j + D])
                acc = v if acc is None else acc + v
            gdls[j, g] = acc.reshape(4, 64, D).astype(BF)
    dlx = (2, gdls, r1_dl, p2s_dl, p2r_dl, gdl_o)
    scatter_y(*dlx[:3])

    add_y(*dr)
    add_y(*ulx)
    add_y(*dlx)

    def in_wait(c, _):
        wait_recv(3, c, recv_d)
        in_stage(c, 0)
        return 0

    lax.fori_loop(0, NC - 1, in_wait, 0)
    add_z(*dr)
    add_z(*ulx)
    add_z(*dlx)
    wait_recv(3, NC - 1, recv_d)
    for l in range(NB):
        acc = None
        for c in range(NC):
            v = mm_nt(tokt[c, D * l:D * l + D, :], recv_d[c, :, l].reshape(H, R))
            acc = v if acc is None else acc + v
        gurs[l] = acc.reshape(8, 16, H).astype(BF)

    def ur_send(k, _):
        p = lax.rem(dp + k, 8)
        pltpu.make_async_remote_copy(
            src_ref=gurs.at[:, p], dst_ref=r_ur.at[k - 1],
            send_sem=sur.at[k - 1], recv_sem=qur.at[k - 1],
            device_id={"dp": p}, device_id_type=pl.DeviceIdType.MESH,
        ).start()
        return 0

    lax.fori_loop(1, 8, ur_send, 0)
    in_stage(NC - 1, 0)

    def drain(c, _):
        wait_send(1, c, send_a)
        wait_send(3, c, send_c)
        return 0

    lax.fori_loop(0, NC, drain, 0)
    for k in range(7):
        pltpu.make_async_copy(r_ur.at[k], r_ur.at[k], qur.at[k]).wait()
    for l in range(NB):
        t = gurs[l, dp].astype(F32)
        for k in range(7):
            t = t + r_ur[k, l].astype(F32)
        gur_o[l] = t
    for k in range(7):
        pltpu.make_async_copy(r_ur.at[k], r_ur.at[k], sur.at[k]).wait()


def per_device(tokens, up_first_weight, up_left, down_first_weight, down_left, out_grad):
    vm = pl.BlockSpec(memory_space=pltpu.VMEM)
    big = (NC, ND, NB, 32, R)
    outs = (
        jax.ShapeDtypeStruct((NC * R, NB * D), BF),
        jax.ShapeDtypeStruct((NC * R, NB * D), BF),
        jax.ShapeDtypeStruct((NB, D // 8, H), F32),
        jax.ShapeDtypeStruct((NB, H // 8, H), F32),
        jax.ShapeDtypeStruct((NB, H // 8, H), F32),
        jax.ShapeDtypeStruct((NB, H // 8, D), F32),
    )
    scratch = [
        pltpu.VMEM((NB, H, D), BF),
        pltpu.VMEM((NB, 2, 4, 64, H), BF),
        pltpu.VMEM((NB, 2, 4, 64, H), BF),
        pltpu.VMEM((NB, D, H), BF),
        pltpu.VMEM((NC, NB * D, R), BF),
    ]
    scratch += [pltpu.VMEM(big, BF)] * 6
    scratch += [pltpu.VMEM((NC, NB, H, R), BF)] * 2
    scratch += [
        pltpu.VMEM((NB, 2, 4, 64, D), BF),
        pltpu.VMEM((NB, 8, 16, H), BF),
        pltpu.VMEM((3, NB, 2, 64, H), BF),
        pltpu.VMEM((3, NB, 2, 64, H), BF),
        pltpu.VMEM((3, NB, 2, 64, D), BF),
        pltpu.VMEM((7, NB, 16, H), BF),
    ]
    scratch += [pltpu.VMEM((NB, 64, n), BF) for n in (H, H, D, H, H, D)]
    dma = pltpu.SemaphoreType.DMA
    scratch += [dma((4, NC)), dma((4, NC)), dma((3, 3)), dma((3, 3)), dma((3,)), dma((3,)), dma((7,)), dma((7,))]
    return pl.pallas_call(
        kernel,
        out_shape=outs,
        in_specs=[vm] * 6,
        out_specs=[vm] * 6,
        scratch_shapes=scratch,
        compiler_params=pltpu.CompilerParams(
            collective_id=0, has_side_effects=True, vmem_limit_bytes=63 * 2**20
        ),
        cost_estimate=pl.CostEstimate(flops=2 * 8053063680, bytes_accessed=11 * 2**20, transcendentals=2**21),
        name="monarch",
    )(tokens, up_first_weight, up_left, down_first_weight, down_left, out_grad)


def solution(mesh):
    return jax.shard_map(
        per_device,
        mesh=mesh,
        in_specs=(
            P("dp", "tensor"),
            P("tensor", None, None),
            P("tensor", None, None),
            P("tensor", None, None),
            P("tensor", None, None),
            P("dp", "tensor"),
        ),
        out_specs=(
            P("dp", "tensor"),
            P("dp", "tensor"),
            P("tensor", "dp", None),
            P("tensor", "dp", None),
            P("tensor", "dp", None),
            P("tensor", "dp", None),
        ),
        check_vma=False,
    )
```

time: 497 us -> 225 us (0.45)
  waiting for transfers between devices: 316 us -> 0 us
  Pallas kernels: 0 us -> 218 us
  matrix products: 73.9 us -> 0 us
  starting transfers between devices: 49 us -> 0 us
  local copies, waits for them, and re-layouts: 34.4 us -> 6.27 us
  between operations: 14.8 us -> 0.67 us
    pallas_call x0 -> x1, Pallas kernels: none -> 218 us  [per_device(): pl.pallas_call(kernel, out_shape=outs, in_specs=[vm] * 6, out_specs=[vm]...]
    all_to_all x4 -> x0, waiting for transfers between devices: 186 us -> none  [the longest x1 53.5 us: per_device(): lax.all_to_all(second_factor.reshape(out_shape), 'tensor', split_axis=2,...]
    reduce_scatter x3 -> x0, waiting for transfers between devices: 130 us -> none  [the longest x1 59.7 us: per_device(): lax.psum_scatter(grad_ul, 'dp', scatter_dimension=1, tiled=True)]
    dot_general x12 -> x0, matrix products: 73.9 us -> none  [the longest x1 10.9 us: per_device(): jnp.einsum('rln,rlm->lnm', hidden_state, second_grad, preferred_element_t...]
    all_to_all x4 -> x0, starting transfers between devices: 48.5 us -> none  [the longest x1 13.4 us: per_device(): lax.all_to_all(grad_mixed_down.reshape(back_shape), 'tensor', split_axis=...]
    reshape x7 -> x0, local copies, waits for them, and re-layouts: 19.1 us -> none  [the longest x1 4.3 us: per_device(): grad_mixed_up.reshape(back_shape)]
    all_to_all x2 -> x0, local copies, waits for them, and re-layouts: 5.54 us -> none  [the longest x1 2.83 us: per_device(): lax.all_to_all(grad_mixed_down.reshape(back_shape), 'tensor', split_axis=...]
  transfers between devices with their start and end apart: 8 -> 0, of which waited for: 7 -> 0; matrix products, arithmetic and copies ran while one was open for 17% -> 0% of each run, Pallas kernels for 0% -> 0%
where the time goes in v1:
time: 225 us
  Pallas kernels  218 us (97%)
  local copies, waits for them, and re-layouts  6.27 us (3%)
    pallas_call x1, Pallas kernels, per_device(): pl.pallas_call(kernel, out_shape=outs, in_specs=[vm] * 6, out_specs=[vm]...  218 us
    unnamed x16, local copies, waits for them, and re-layouts  6.27 us

profile of v1, /device:TPU:1, one launch (start us, length us, event | category | flops | bytes accessed | tf_op | source)
XLA Modules:
  0.0 224.5 jit_solution(8121907919352947391)
XLA Ops:
  0.6 217.6 %monarch.1 = (bf16[1024,512]{1,0:T(8,128)(2,1)}, bf16[1024,512]{1,0:T(8,128)(2,1)}, f32[4,16,512]{2,1,0:T(8,128)}, f32[4,64,512]{2,1,0:T(8,128)}, f32[4,64,512]{2,1,0:T(8,128)}, /*index=5*/f32[4,64,128]{2,1,0:T(8,128)}) custom-call(bf16[1024,512]{1,0:T(8,128)(2,1)} %tok.1, bf16[4,128,512]{2,1,0:T(8,128)(2,1)} %w1.1, bf16[4,512,512]{2,1,0:T(8,128)(2,1)} %ul.1, ...), custom_call_target="tpu_custom_call" | custom-call | flops 16106127360 | bytes 11534336 | tf_op jit(solution)/shard_map/monarch/pallas_call | solution.py:329
  218.2 0.0 copy-start
  218.2 0.0 copy-start.4
  218.2 0.0 copy-start.2
  218.2 2.4 %copy.18 = bf16[1024,512]{1,0:T(8,128)(2,1)} copy(bf16[1024,512]{1,0:T(8,128)(2,1)} %get-tuple-element.12) | data formatting | bytes 2097152
  220.6 0.0 copy-done
  220.6 0.0 copy-start.1
  220.6 0.0 copy-start.3
  220.6 1.0 copy.19
  221.6 0.0 copy-done.4
  221.6 0.7 copy.20
  222.3 0.0 copy-done.2
  222.3 0.8 copy.21
  223.1 0.0 copy-done.1
  223.1 0.8 copy.22
  223.8 0.0 copy-done.3
  223.9 0.7 copy.23
Async XLA Ops:
  218.2 2.4 %copy-start = (bf16[1024,512]{1,0:T(8,128)(2,1)S(1)}, bf16[1024,512]{1,0:T(8,128)(2,1)}, u32[]{:S(2)}) copy-start(bf16[1024,512]{1,0:T(8,128)(2,1)} %get-tuple-element.13) | copy-start | bytes 3145732
  218.2 3.4 %copy-start.4 = (f32[4,16,512]{2,1,0:T(8,128)S(1)}, f32[4,16,512]{2,1,0:T(8,128)}, u32[]{:S(2)}) copy-start(f32[4,16,512]{2,1,0:T(8,128)} %get-tuple-element.14) | copy-start | bytes 393220
  218.2 4.0 %copy-start.2 = (f32[4,64,512]{2,1,0:T(8,128)S(1)}, f32[4,64,512]{2,1,0:T(8,128)}, u32[]{:S(2)}) copy-start(f32[4,64,512]{2,1,0:T(8,128)} %get-tuple-element.15) | copy-start | bytes 1572868
  220.6 2.4 %copy-start.1 = (f32[4,64,512]{2,1,0:T(8,128)S(1)}, f32[4,64,512]{2,1,0:T(8,128)}, u32[]{:S(2)}) copy-start(f32[4,64,512]{2,1,0:T(8,128)} %get-tuple-element.16) | copy-start | bytes 1572868
  220.6 3.2 %copy-start.3 = (f32[4,64,128]{2,1,0:T(8,128)S(1)}, f32[4,64,128]{2,1,0:T(8,128)}, u32[]{:S(2)}) copy-start(f32[4,64,128]{2,1,0:T(8,128)} %get-tuple-element.17) | copy-start | bytes 393220

commit v2 on v1

--- a/solution.py
+++ b/solution.py
@@ -26,13 +26,14 @@
 
 
 def kernel(
+    tok_h, w1_h, ul_h, df_h, dl_h, og_h,
+    lo, ig, gur_o, gul_o, gdr_o, gdl_o,
     tok, w1, ul, df, dl, og,
-    lo, ig, gur_o, gul_o, gdr_o, gdl_o,
-    w1t, ult, dft, dlt, tokt,
+    w1t, pw1, pdl, ptok, pog, ult, dft, dlt,
     recv_a, recv_b, recv_c, recv_d, send_a, send_c, hid, dgel,
     gdls, gurs, r1_ul, r1_dr, r1_dl, r_ur,
     p2s_ul, p2s_dr, p2s_dl, p2r_ul, p2r_dr, p2r_dl,
-    ssem, rsem, s1, q1, s2, q2, sur, qur,
+    ld, ssem, rsem, sx, qx, sv, qv, sf, qf, qd, s1, q1, s2, q2, sur, qur,
 ):
     me = lax.axis_index("tensor")
     dp = lax.axis_index("dp")
@@ -40,6 +41,36 @@
     zl = dp // 4
     zo = 1 - zl
 
+    mx = me // 4
+    zc = lax.rem(me, 4)
+    mz = zc // 2
+    mc = lax.rem(zc, 2)
+    mate_z = me + 2 - 4 * mz
+    odd = lax.rem(mx, 2)
+    turn = lax.rem((mx + 1) // 2, 2)
+
+    def pair(s, a, b):
+        return (1 - s) * a + s * b
+
+    def mate_x(s):
+        return 4 * pair(s, mx + 1 - 2 * odd, 3 - mx) + zc
+
+    def own_x(s, h):
+        return pair(s, turn + h * (3 - 2 * turn), mx - odd + h)
+
+    def mate_serves(s, h):
+        return pair(s, 1 - turn + h * (1 + 2 * turn), 2 - mx + odd + h)
+
+    def own_place(s):
+        return pair(s, mx // 2, odd)
+
+    loads = [
+        pltpu.make_async_copy(a, b, ld.at[i])
+        for i, (a, b) in enumerate(((dl_h, dl), (og_h, og), (w1_h, w1), (tok_h, tok), (ul_h, ul), (df_h, df)))
+    ]
+    for load in loads:
+        load.start()
+
     barrier = pltpu.get_barrier_semaphore()
 
     def greet_t(k, _):
@@ -53,9 +84,55 @@
     lax.fori_loop(1, ND, greet_t, 0)
     lax.fori_loop(1, 8, greet_d, 0)
 
-    for l in range(NB):
-        w1t[l] = w1[l].T
     pl.semaphore_wait(barrier, ND - 1 + 7)
+
+    def remote(src, dst, ss, rs, **where):
+        return pltpu.make_async_remote_copy(
+            src_ref=src, dst_ref=dst, send_sem=ss, recv_sem=rs,
+            device_id=where, device_id_type=pl.DeviceIdType.MESH,
+        )
+
+    def arrived(view, sem):
+        pltpu.make_async_copy(view, view, sem).wait()
+
+    def dl_slices(s):
+        return [remote(dl.at[y, mate_serves(s, h)], pdl.at[s, y, h], sv.at[s], qv.at[s], tensor=mate_x(s)) for h in range(2)]
+
+    def w1_slice():
+        return remote(w1t.at[y, :, 1 - mz], pw1.at[y], sv.at[2], qv.at[2], tensor=mate_z)
+
+    def hand_on(i, buf):
+        return [
+            remote(buf.at[y], buf.at[y], sf.at[i, k - 1], qf.at[i, k - 1], dp=zl * 4 + lax.rem(y + k, 4))
+            for k in range(1, 4)
+        ]
+
+    def pass_on(i, buf):
+        arrived(buf.at[y], qv.at[i])
+        for copy in hand_on(i, buf):
+            copy.start()
+
+    def passed(i, buf):
+        for k in range(1, 4):
+            arrived(buf.at[lax.rem(y - k + 4, 4)], qf.at[i, k - 1])
+
+    def sent_slices():
+        for s in range(2):
+            arrived(pdl.at[s, 0], sv.at[s])
+        w1_slice().wait_send()
+        for i, buf in ((0, pdl.at[0]), (1, pdl.at[1]), (2, pw1)):
+            for copy in hand_on(i, buf):
+                copy.wait_send()
+
+    def rows_to_mate(i, c, src, dst, mate):
+        view = pl.ds(pl.multiple_of(c * R, R), R)
+        return remote(src.at[view], dst.at[c], sx.at[i, c], qx.at[i, c], tensor=mate)
+
+    def og_copy(c):
+        return rows_to_mate(0, c, og, pog, mate_x(lax.rem(c, 2)))
+
+    def tok_copy(c):
+        return rows_to_mate(1, c, tok, ptok, mate_z)
 
     def send(ph, c, sbuf, rbuf):
         def one(k, _):
@@ -73,8 +150,8 @@
     def wait_recv(ph, c, rbuf):
         pltpu.make_async_copy(rbuf.at[c], rbuf.at[c], rsem.at[ph, c]).wait()
 
-    def wait_send(ph, c, sbuf):
-        view = sbuf.at[c, pl.ds(0, ND - 1)]
+    def wait_send(ph, c, sbuf, n=ND - 1):
+        view = sbuf.at[c, pl.ds(0, n)]
         pltpu.make_async_copy(view, view, ssem.at[ph, c]).wait()
 
     def rows(c):
@@ -83,24 +160,65 @@
     def pack(parts, axis, shape):
         return jnp.concatenate([p.reshape(shape) for p in parts], axis=axis).reshape(8, NB, 32, R).astype(BF)
 
+    def tiles(parts, n):
+        return jnp.concatenate([p.reshape(8 * n // 2, 1, 8, R) for p in parts], axis=1).reshape(n, NB, 32, R).astype(BF)
+
+    def first_plain(c):
+        for g in range(2):
+            parts = [
+                mm_nt(w1t[l, 2 * g:2 * g + 2].reshape(256, D), tok[R * c:R * c + R, D * l:D * l + D]) for l in range(NB)
+            ]
+            send_a[c, 8 * g:8 * g + 8] = tiles(parts, 8)
+        send(0, c, send_a, recv_a)
+
+    def to_eight(ph, c, sbuf, rbuf, mate, place, target):
+        def one(i, _):
+            k = lax.rem(place + i, 8)
+            for half, src in ((0, me), (8, mate)):
+                remote(
+                    sbuf.at[c, half + k], rbuf.at[c, src], ssem.at[ph, c], rsem.at[ph, c], tensor=target(k)
+                ).start()
+            return 0
+
+        for half, src in ((0, me), (8, mate)):
+            pltpu.make_async_copy(sbuf.at[c, half + place], rbuf.at[c, src], rsem.at[ph, c]).start()
+        lax.fori_loop(1, 8, one, 0)
+
     def first_stage(c, _):
-        tokt[c] = tok[rows(c), :].T
-        for g in range(2):
-            parts = [mm(w1t[l, 256 * g:256 * g + 256, :], tokt[c, D * l:D * l + D, :]) for l in range(NB)]
-            send_a[c, 8 * g:8 * g + 8] = pack(parts, 1, (32, 1, 8, R))
-        send(0, c, send_a, recv_a)
+        parts = [mm_nt(w1t[l, :, mz].reshape(256, D), tok[rows(c), D * l:D * l + D]) for l in range(NB)]
+        send_a[c, 0:8] = tiles(parts, 8)
+        arrived(ptok.at[c], qx.at[1, c])
+        parts = [mm_nt(pw1[l].reshape(256, D), ptok[c, :, D * l:D * l + D]) for l in range(NB)]
+        send_a[c, 8:16] = tiles(parts, 8)
+        to_eight(0, c, send_a, recv_a, mate_z, 2 * mx + mc, lambda k: 4 * (k // 2) + 2 * mz + lax.rem(k, 2))
         return 0
 
     def gmd_stage(c, _):
-        for g in range(2):
-            parts = [mm_nt(dl[j, 256 * g:256 * g + 256, :], og[rows(c), D * j:D * j + D]) for j in range(NB)]
-            send_c[c, 8 * g:8 * g + 8] = pack(parts, 2, (8, 4, 1, 8, R))
-        send(2, c, send_c, recv_c)
+        s = lax.rem(c, 2)
+        for h in range(2):
+            parts = [mm_nt(dl[j, own_x(s, h)], og[rows(c), D * j:D * j + D]) for j in range(NB)]
+            send_c[c, 4 * h:4 * h + 4] = tiles(parts, 4)
+        arrived(pog.at[c], qx.at[0, c])
+        for h in range(2):
+            parts = [mm_nt(pdl[s, j, h], pog[c, :, D * j:D * j + D]) for j in range(NB)]
+            send_c[c, 8 + 4 * h:12 + 4 * h] = tiles(parts, 4)
+        to_eight(
+            2, c, send_c, recv_c, mate_x(s), 4 * own_place(s) + zc,
+            lambda k: 4 * own_x(s, k // 4) + lax.rem(k, 4),
+        )
         return 0
 
     def mid_stage(c, _):
         wait_recv(0, c, recv_a)
-        wait_send(0, c, send_a)
+
+        @pl.when(c == 0)
+        def _():
+            wait_send(0, c, send_a)
+
+        @pl.when(c > 0)
+        def _():
+            wait_send(0, c, send_a, ND - 2)
+
 
         def act(j, _):
             x = mm(ult[j].reshape(H, H), recv_a[c, :, j].reshape(H, R))
@@ -121,7 +239,7 @@
 
     def back_stage(c, _):
         wait_recv(2, c, recv_c)
-        wait_send(2, c, send_c)
+        wait_send(2, c, send_c, ND - 2)
 
         def act(l, _):
             hg = mm(df[l], recv_c[c, :, l].reshape(H, R))
@@ -132,7 +250,28 @@
         for g in range(2):
             parts = [mm(ul[j, 256 * g:256 * g + 256, :], dgel[c, j]) for j in range(NB)]
             send_c[c, 8 * g:8 * g + 8] = pack(parts, 2, (8, 4, 1, 8, R))
-        send(3, c, send_c, recv_d)
+
+        @pl.when(c < NC - 2)
+        def _():
+            send(3, c, send_c, recv_d)
+
+        return 0
+
+    def send_last(l, _):
+        for c in (NC - 2, NC - 1):
+            pltpu.make_async_copy(send_c.at[c, me, l], recv_d.at[c, me, l], qd.at[c - NC + 2, l]).start()
+
+        def one(k, _):
+            p = lax.rem(me + k, ND)
+            for c in (NC - 2, NC - 1):
+                pltpu.make_async_remote_copy(
+                    src_ref=send_c.at[c, p, l], dst_ref=recv_d.at[c, me, l],
+                    send_sem=ssem.at[3, c], recv_sem=qd.at[c - NC + 2, l],
+                    device_id={"tensor": p}, device_id_type=pl.DeviceIdType.MESH,
+                ).start()
+            return 0
+
+        lax.fori_loop(1, ND, one, 0)
         return 0
 
     def out_stage(c, _):
@@ -142,10 +281,13 @@
             lo[rows(c), D * j:D * j + D] = (tok[rows(c), D * j:D * j + D].astype(F32) + b.T).astype(BF)
         return 0
 
+    def in_block(c, l):
+        b = mm(w1[l], recv_d[c, :, l].reshape(H, R))
+        ig[rows(c), D * l:D * l + D] = (og[rows(c), D * l:D * l + D].astype(F32) + b.T).astype(BF)
+
     def in_stage(c, _):
         for l in range(NB):
-            b = mm(w1[l], recv_d[c, :, l].reshape(H, R))
-            ig[rows(c), D * l:D * l + D] = (og[rows(c), D * l:D * l + D].astype(F32) + b.T).astype(BF)
+            in_block(c, l)
         return 0
 
     def scatter_y(i, gs, r1):
@@ -190,8 +332,29 @@
         for k in range(1, 4):
             pltpu.make_async_copy(r1.at[k - 1], r1.at[k - 1], s1.at[i, k - 1]).wait()
 
-    lax.fori_loop(0, NC, first_stage, 0)
-    lax.fori_loop(0, NC, gmd_stage, 0)
+    loads[0].wait()
+    for s in range(2):
+        for copy in dl_slices(s):
+            copy.start()
+    loads[1].wait()
+    og_copy(0).start()
+    og_copy(1).start()
+    loads[2].wait()
+    for l in range(NB):
+        w1t[l] = w1[l].T.reshape(4, 2, 64, D)
+    w1_slice().start()
+    loads[3].wait()
+    tok_copy(1).start()
+    first_plain(0)
+    pass_on(0, pdl.at[0])
+    pass_on(1, pdl.at[1])
+    pass_on(2, pw1)
+    og_copy(2).start()
+    og_copy(3).start()
+    tok_copy(2).start()
+    tok_copy(3).start()
+    loads[4].wait()
+    loads[5].wait()
 
     def prep(l, _):
         u = ul[l].T
@@ -200,12 +363,20 @@
         v = df[l].T
         dft[l, 0] = v[0:256].reshape(4, 64, H)
         dft[l, 1] = v[256:512].reshape(4, 64, H)
-        dlt[l] = dl[l].T
+        dlt[l] = dl[l].reshape(H, D).T
         return 0
 
     lax.fori_loop(0, NB, prep, 0)
+    passed(0, pdl.at[0])
+    passed(1, pdl.at[1])
+    lax.fori_loop(0, 2, gmd_stage, 0)
+    passed(2, pw1)
+    first_stage(1, 0)
+    lax.fori_loop(2, NC, gmd_stage, 0)
+    lax.fori_loop(2, NC, first_stage, 0)
     lax.fori_loop(0, NC, mid_stage, 0)
     lax.fori_loop(0, NC, back_stage, 0)
+    lax.fori_loop(0, NB, send_last, 0)
 
     def grad_right(l, _):
         for g in range(2):
@@ -254,29 +425,32 @@
         in_stage(c, 0)
         return 0
 
-    lax.fori_loop(0, NC - 1, in_wait, 0)
+    lax.fori_loop(0, NC - 2, in_wait, 0)
     add_z(*dr)
     add_z(*ulx)
     add_z(*dlx)
-    wait_recv(3, NC - 1, recv_d)
+
+    def ur_copy(l, k):
+        p = lax.rem(dp + k, 8)
+        return pltpu.make_async_remote_copy(
+            src_ref=gurs.at[l, p], dst_ref=r_ur.at[l, k - 1],
+            send_sem=sur.at[l, k - 1], recv_sem=qur.at[l, k - 1],
+            device_id={"dp": p}, device_id_type=pl.DeviceIdType.MESH,
+        )
+
     for l in range(NB):
+        for c in (NC - 2, NC - 1):
+            view = recv_d.at[c, :, l]
+            pltpu.make_async_copy(view, view, qd.at[c - NC + 2, l]).wait()
         acc = None
         for c in range(NC):
-            v = mm_nt(tokt[c, D * l:D * l + D, :], recv_d[c, :, l].reshape(H, R))
+            v = mm(recv_d[c, :, l].reshape(H, R), tok[R * c:R * c + R, D * l:D * l + D])
             acc = v if acc is None else acc + v
-        gurs[l] = acc.reshape(8, 16, H).astype(BF)
-
-    def ur_send(k, _):
-        p = lax.rem(dp + k, 8)
-        pltpu.make_async_remote_copy(
-            src_ref=gurs.at[:, p], dst_ref=r_ur.at[k - 1],
-            send_sem=sur.at[k - 1], recv_sem=qur.at[k - 1],
-            device_id={"dp": p}, device_id_type=pl.DeviceIdType.MESH,
-        ).start()
-        return 0
-
-    lax.fori_loop(1, 8, ur_send, 0)
-    in_stage(NC - 1, 0)
+        gurs[l] = acc.T.reshape(8, 16, H).astype(BF)
+        for k in range(1, 8):
+            ur_copy(l, k).start()
+        for c in (NC - 2, NC - 1):
+            in_block(c, l)
 
     def drain(c, _):
         wait_send(1, c, send_a)
@@ -284,19 +458,38 @@
         return 0
 
     lax.fori_loop(0, NC, drain, 0)
-    for k in range(7):
-        pltpu.make_async_copy(r_ur.at[k], r_ur.at[k], qur.at[k]).wait()
+    sent_slices()
+    for c in range(NC):
+        og_copy(c).wait_send()
+        if c > 0:
+            tok_copy(c).wait_send()
     for l in range(NB):
+        for k in range(1, 8):
+            ur_copy(l, k).wait_recv()
         t = gurs[l, dp].astype(F32)
         for k in range(7):
-            t = t + r_ur[k, l].astype(F32)
+            t = t + r_ur[l, k].astype(F32)
         gur_o[l] = t
-    for k in range(7):
-        pltpu.make_async_copy(r_ur.at[k], r_ur.at[k], sur.at[k]).wait()
+        for k in range(1, 8):
+            ur_copy(l, k).wait_send()
+
+
+def hand_over(*refs):
+    srcs, dsts, bufs, s_in, s_out = refs[:6], refs[6:12], refs[12:18], refs[18], refs[19]
+    ins = [pltpu.make_async_copy(a, b, s_in.at[i]) for i, (a, b) in enumerate(zip(srcs, bufs))]
+    outs = [pltpu.make_async_copy(a, b, s_out.at[i]) for i, (a, b) in enumerate(zip(bufs, dsts))]
+    for copy in ins:
+        copy.start()
+    for i in range(6):
+        ins[i].wait()
+        outs[i].start()
+    for copy in outs:
+        copy.wait()
 
 
 def per_device(tokens, up_first_weight, up_left, down_first_weight, down_left, out_grad):
     vm = pl.BlockSpec(memory_space=pltpu.VMEM)
+    anywhere = pl.BlockSpec(memory_space=pl.ANY)
     big = (NC, ND, NB, 32, R)
     outs = (
         jax.ShapeDtypeStruct((NC * R, NB * D), BF),
@@ -307,11 +500,20 @@
         jax.ShapeDtypeStruct((NB, H // 8, D), F32),
     )
     scratch = [
-        pltpu.VMEM((NB, H, D), BF),
+        pltpu.VMEM((NC * R, NB * D), BF),
+        pltpu.VMEM((NB, D, H), BF),
+        pltpu.VMEM((NB, H, H), BF),
+        pltpu.VMEM((NB, H, H), BF),
+        pltpu.VMEM((NB, 4, D, D), BF),
+        pltpu.VMEM((NC * R, NB * D), BF),
+        pltpu.VMEM((NB, 4, 2, 64, D), BF),
+        pltpu.VMEM((NB, 4, 64, D), BF),
+        pltpu.VMEM((2, NB, 2, D, D), BF),
+        pltpu.VMEM((NC, R, NB * D), BF),
+        pltpu.VMEM((NC, R, NB * D), BF),
         pltpu.VMEM((NB, 2, 4, 64, H), BF),
         pltpu.VMEM((NB, 2, 4, 64, H), BF),
         pltpu.VMEM((NB, D, H), BF),
-        pltpu.VMEM((NC, NB * D, R), BF),
     ]
     scratch += [pltpu.VMEM(big, BF)] * 6
     scratch += [pltpu.VMEM((NC, NB, H, R), BF)] * 2
@@ -321,15 +523,16 @@
         pltpu.VMEM((3, NB, 2, 64, H), BF),
         pltpu.VMEM((3, NB, 2, 64, H), BF),
         pltpu.VMEM((3, NB, 2, 64, D), BF),
-        pltpu.VMEM((7, NB, 16, H), BF),
+        pltpu.VMEM((NB, 7, 16, H), BF),
     ]
     scratch += [pltpu.VMEM((NB, 64, n), BF) for n in (H, H, D, H, H, D)]
     dma = pltpu.SemaphoreType.DMA
-    scratch += [dma((4, NC)), dma((4, NC)), dma((3, 3)), dma((3, 3)), dma((3,)), dma((3,)), dma((7,)), dma((7,))]
-    return pl.pallas_call(
+    scratch += [dma((6,)), dma((4, NC)), dma((4, NC)), dma((2, NC)), dma((2, NC))]
+    scratch += [dma((3,)), dma((3,)), dma((3, 3)), dma((3, 3)), dma((2, NB)), dma((3, 3)), dma((3, 3)), dma((3,)), dma((3,)), dma((NB, 7)), dma((NB, 7))]
+    results = pl.pallas_call(
         kernel,
         out_shape=outs,
-        in_specs=[vm] * 6,
+        in_specs=[anywhere] * 6,
         out_specs=[vm] * 6,
         scratch_shapes=scratch,
         compiler_params=pltpu.CompilerParams(
@@ -337,7 +540,16 @@
         ),
         cost_estimate=pl.CostEstimate(flops=2 * 8053063680, bytes_accessed=11 * 2**20, transcendentals=2**21),
         name="monarch",
-    )(tokens, up_first_weight, up_left, down_first_weight, down_left, out_grad)
+    )(tokens, up_first_weight, up_left, down_first_weight, down_left.reshape(NB, 4, D, D), out_grad)
+    return pl.pallas_call(
+        hand_over,
+        out_shape=outs,
+        in_specs=[anywhere] * 6,
+        out_specs=[anywhere] * 6,
+        scratch_shapes=[pltpu.VMEM(o.shape, o.dtype) for o in outs] + [dma((6,)), dma((6,))],
+        compiler_params=pltpu.CompilerParams(vmem_limit_bytes=63 * 2**20),
+        name="hand_over",
+    )(*results)
 
 
 def solution(mesh):

time: 225 us -> 210 us (0.933)
  Pallas kernels: 218 us -> 210 us
  local copies, waits for them, and re-layouts: 6.27 us -> 0 us
    pallas_call x1 -> x2, Pallas kernels: 218 us -> 210 us  [the longest x1 207 us: per_device(): pl.pallas_call(kernel, out_shape=outs, in_specs=[anywhere] * 6, out_specs...]
    unnamed x16 -> x0, local copies, waits for them, and re-layouts: 6.27 us -> none
where the time goes in v2:
time: 210 us
  Pallas kernels  210 us (100%)
    pallas_call x1, Pallas kernels, per_device(): pl.pallas_call(kernel, out_shape=outs, in_specs=[anywhere] * 6, out_specs...  207 us

profile of v2, /device:TPU:1, one launch (start us, length us, event | category | flops | bytes accessed | tf_op | source)
XLA Modules:
  0.0 210.2 jit_solution(13459906635493892024)
XLA Ops:
  0.6 206.5 %monarch.1 = (bf16[1024,512]{1,0:T(8,128)(2,1)}, bf16[1024,512]{1,0:T(8,128)(2,1)}, f32[4,16,512]{2,1,0:T(8,128)}, f32[4,64,512]{2,1,0:T(8,128)}, f32[4,64,512]{2,1,0:T(8,128)}, /*index=5*/f32[4,64,128]{2,1,0:T(8,128)}) custom-call(bf16[1024,512]{1,0:T(8,128)(2,1)} %tok_h.1, bf16[4,128,512]{2,1,0:T(8,128)(2,1)} %w1_h.1, bf16[4,512,512]{2,1,0:T(8,128)(2,1)} %ul_h.1, ...), custom_call_target="tpu_custom_call" | custom-call | flops 16106127360 | bytes 11534336 | tf_op jit(solution)/shard_map/monarch/pallas_call | solution.py:532
  207.2 3.1 %hand_over.1 = (bf16[1024,512]{1,0:T(8,128)(2,1)}, bf16[1024,512]{1,0:T(8,128)(2,1)}, f32[4,16,512]{2,1,0:T(8,128)}, f32[4,64,512]{2,1,0:T(8,128)}, f32[4,64,512]{2,1,0:T(8,128)}, /*index=5*/f32[4,64,128]{2,1,0:T(8,128)}) custom-call(bf16[1024,512]{1,0:T(8,128)(2,1)} %get-tuple-element.12.refs_0_, bf16[1024,512]{1,0:T(8,128)(2,1)} %get-tuple-element.13.refs_1_, ...), custom_call_target="tpu_custom_call" | custom-call | tf_op jit(solution)/shard_map/hand_over/pallas_call | solution.py:544

commit v3 on v2

--- a/solution.py
+++ b/solution.py
@@ -353,8 +353,6 @@
     og_copy(3).start()
     tok_copy(2).start()
     tok_copy(3).start()
-    loads[4].wait()
-    loads[5].wait()
 
     def prep(l, _):
         u = ul[l].T
@@ -366,7 +364,6 @@
         dlt[l] = dl[l].reshape(H, D).T
         return 0
 
-    lax.fori_loop(0, NB, prep, 0)
     passed(0, pdl.at[0])
     passed(1, pdl.at[1])
     lax.fori_loop(0, 2, gmd_stage, 0)
@@ -374,6 +371,9 @@
     first_stage(1, 0)
     lax.fori_loop(2, NC, gmd_stage, 0)
     lax.fori_loop(2, NC, first_stage, 0)
+    loads[4].wait()
+    loads[5].wait()
+    lax.fori_loop(0, NB, prep, 0)
     lax.fori_loop(0, NC, mid_stage, 0)
     lax.fori_loop(0, NC, back_stage, 0)
     lax.fori_loop(0, NB, send_last, 0)
@@ -426,9 +426,6 @@
         return 0
 
     lax.fori_loop(0, NC - 2, in_wait, 0)
-    add_z(*dr)
-    add_z(*ulx)
-    add_z(*dlx)
 
     def ur_copy(l, k):
         p = lax.rem(dp + k, 8)
@@ -457,6 +454,9 @@
         wait_send(3, c, send_c)
         return 0
 
+    add_z(*dr)
+    add_z(*ulx)
+    add_z(*dlx)
     lax.fori_loop(0, NC, drain, 0)
     sent_slices()
     for c in range(NC):
@@ -475,14 +475,10 @@
 
 
 def hand_over(*refs):
-    srcs, dsts, bufs, s_in, s_out = refs[:6], refs[6:12], refs[12:18], refs[18], refs[19]
-    ins = [pltpu.make_async_copy(a, b, s_in.at[i]) for i, (a, b) in enumerate(zip(srcs, bufs))]
-    outs = [pltpu.make_async_copy(a, b, s_out.at[i]) for i, (a, b) in enumerate(zip(bufs, dsts))]
-    for copy in ins:
+    srcs, dsts, s_out = refs[:6], refs[6:12], refs[12]
+    outs = [pltpu.make_async_copy(a, b, s_out.at[i]) for i, (a, b) in enumerate(zip(srcs, dsts))]
+    for copy in outs:
         copy.start()
-    for i in range(6):
-        ins[i].wait()
-        outs[i].start()
     for copy in outs:
         copy.wait()
 
@@ -531,12 +527,12 @@
     scratch += [dma((3,)), dma((3,)), dma((3, 3)), dma((3, 3)), dma((2, NB)), dma((3, 3)), dma((3, 3)), dma((3,)), dma((3,)), dma((NB, 7)), dma((NB, 7))]
     results = pl.pallas_call(
         kernel,
-        out_shape=outs,
+        out_shape=[pltpu.VMEM(o.shape, o.dtype) for o in outs],
         in_specs=[anywhere] * 6,
         out_specs=[vm] * 6,
         scratch_shapes=scratch,
         compiler_params=pltpu.CompilerParams(
-            collective_id=0, has_side_effects=True, vmem_limit_bytes=63 * 2**20
+            collective_id=0, has_side_effects=True, vmem_limit_bytes=60 * 2**20
         ),
         cost_estimate=pl.CostEstimate(flops=2 * 8053063680, bytes_accessed=11 * 2**20, transcendentals=2**21),
         name="monarch",
@@ -544,10 +540,10 @@
     return pl.pallas_call(
         hand_over,
         out_shape=outs,
-        in_specs=[anywhere] * 6,
+        in_specs=[vm] * 6,
         out_specs=[anywhere] * 6,
-        scratch_shapes=[pltpu.VMEM(o.shape, o.dtype) for o in outs] + [dma((6,)), dma((6,))],
-        compiler_params=pltpu.CompilerParams(vmem_limit_bytes=63 * 2**20),
+        scratch_shapes=[dma((6,))],
+        compiler_params=pltpu.CompilerParams(vmem_limit_bytes=2**20),
         name="hand_over",
     )(*results)
 

time: 210 us -> 207 us (0.986)
  Pallas kernels: 210 us -> 207 us
    pallas_call x2, Pallas kernels: 210 us -> 207 us  [the longest x1 205 us: per_device(): pl.pallas_call(kernel, out_shape=[pltpu.VMEM(o.shape, o.dtype) for o in o...]
where the time goes in v3:
time: 207 us
  Pallas kernels  207 us (100%)
    pallas_call x1, Pallas kernels, per_device(): pl.pallas_call(kernel, out_shape=[pltpu.VMEM(o.shape, o.dtype) for o in o...  205 us

profile of v3, /device:TPU:1, one launch (start us, length us, event | category | flops | bytes accessed | tf_op | source)
XLA Modules:
  0.0 207.2 jit_solution(2145722100318452283)
XLA Ops:
  0.6 204.7 %monarch.1 = (bf16[1024,512]{1,0:T(8,128)(2,1)S(1)}, bf16[1024,512]{1,0:T(8,128)(2,1)S(1)}, f32[4,16,512]{2,1,0:T(8,128)S(1)}, f32[4,64,512]{2,1,0:T(8,128)S(1)}...) custom-call(bf16[1024,512]{1,0:T(8,128)(2,1)} %tok_h.1, bf16[4,128,512]{2,1,0:T(8,128)(2,1)} %w1_h.1, ...), custom_call_target="tpu_custom_call" | custom-call | flops 16106127360 | bytes 11534336 | tf_op jit(solution)/shard_map/monarch/pallas_call | solution.py:528
  205.4 1.8 hand_over.1

commit v4 on v3

--- a/solution.py
+++ b/solution.py
@@ -134,18 +134,19 @@
     def tok_copy(c):
         return rows_to_mate(1, c, tok, ptok, mate_z)
 
+    steps = (
+        (1, 0, 0), (0, 1, 0), (3, 0, 0), (1, 1, 0), (3, 1, 0), (2, 0, 0), (0, 1, 1), (2, 1, 0),
+        (1, 0, 1), (3, 0, 1), (1, 1, 1), (3, 1, 1), (2, 0, 1), (2, 1, 1), (0, 0, 1),
+    )
+
+    def step_to(dx, dz, dc):
+        return 4 * lax.rem(mx + dx, 4) + 2 * lax.rem(mz + dz, 2) + lax.rem(mc + dc, 2)
+
     def send(ph, c, sbuf, rbuf):
-        def one(k, _):
-            p = lax.rem(me + k, ND)
-            pltpu.make_async_remote_copy(
-                src_ref=sbuf.at[c, p], dst_ref=rbuf.at[c, me],
-                send_sem=ssem.at[ph, c], recv_sem=rsem.at[ph, c],
-                device_id={"tensor": p}, device_id_type=pl.DeviceIdType.MESH,
-            ).start()
-            return 0
-
         pltpu.make_async_copy(sbuf.at[c, me], rbuf.at[c, me], rsem.at[ph, c]).start()
-        lax.fori_loop(1, ND, one, 0)
+        for step in steps:
+            p = step_to(*step)
+            remote(sbuf.at[c, p], rbuf.at[c, me], ssem.at[ph, c], rsem.at[ph, c], tensor=p).start()
 
     def wait_recv(ph, c, rbuf):
         pltpu.make_async_copy(rbuf.at[c], rbuf.at[c], rsem.at[ph, c]).wait()
@@ -182,6 +183,14 @@
 
         for half, src in ((0, me), (8, mate)):
             pltpu.make_async_copy(sbuf.at[c, half + place], rbuf.at[c, src], rsem.at[ph, c]).start()
+        return one
+
+    def together(*ops):
+        def one(i, _):
+            for op in ops:
+                op(i, 0)
+            return 0
+
         lax.fori_loop(1, 8, one, 0)
 
     def first_stage(c, _):
@@ -190,8 +199,10 @@
         arrived(ptok.at[c], qx.at[1, c])
         parts = [mm_nt(pw1[l].reshape(256, D), ptok[c, :, D * l:D * l + D]) for l in range(NB)]
         send_a[c, 8:16] = tiles(parts, 8)
-        to_eight(0, c, send_a, recv_a, mate_z, 2 * mx + mc, lambda k: 4 * (k // 2) + 2 * mz + lax.rem(k, 2))
-        return 0
+        return 0
+
+    def first_send(c):
+        return to_eight(0, c, send_a, recv_a, mate_z, 2 * mx + mc, lambda k: 4 * (k // 2) + 2 * mz + lax.rem(k, 2))
 
     def gmd_stage(c, _):
         s = lax.rem(c, 2)
@@ -202,11 +213,14 @@
         for h in range(2):
             parts = [mm_nt(pdl[s, j, h], pog[c, :, D * j:D * j + D]) for j in range(NB)]
             send_c[c, 8 + 4 * h:12 + 4 * h] = tiles(parts, 4)
-        to_eight(
+        return 0
+
+    def gmd_send(c):
+        s = lax.rem(c, 2)
+        return to_eight(
             2, c, send_c, recv_c, mate_x(s), 4 * own_place(s) + zc,
             lambda k: 4 * own_x(s, k // 4) + lax.rem(k, 4),
         )
-        return 0
 
     def mid_stage(c, _):
         wait_recv(0, c, recv_a)
@@ -369,8 +383,10 @@
     lax.fori_loop(0, 2, gmd_stage, 0)
     passed(2, pw1)
     first_stage(1, 0)
+    together(gmd_send(0), gmd_send(1), first_send(1))
     lax.fori_loop(2, NC, gmd_stage, 0)
     lax.fori_loop(2, NC, first_stage, 0)
+    together(gmd_send(2), gmd_send(3), first_send(2), first_send(3))
     loads[4].wait()
     loads[5].wait()
     lax.fori_loop(0, NB, prep, 0)
@@ -435,17 +451,18 @@
             device_id={"dp": p}, device_id_type=pl.DeviceIdType.MESH,
         )
 
+    def ur_term(c, l):
+        return mm(recv_d[c, :, l].reshape(H, R), tok[R * c:R * c + R, D * l:D * l + D])
+
     for l in range(NB):
+        acc = ur_term(0, l) + ur_term(1, l)
         for c in (NC - 2, NC - 1):
-            view = recv_d.at[c, :, l]
-            pltpu.make_async_copy(view, view, qd.at[c - NC + 2, l]).wait()
-        acc = None
-        for c in range(NC):
-            v = mm(recv_d[c, :, l].reshape(H, R), tok[R * c:R * c + R, D * l:D * l + D])
-            acc = v if acc is None else acc + v
+            arrived(recv_d.at[c, :, l], qd.at[c - NC + 2, l])
+            acc = acc + ur_term(c, l)
         gurs[l] = acc.T.reshape(8, 16, H).astype(BF)
         for k in range(1, 8):
             ur_copy(l, k).start()
+    for l in range(NB):
         for c in (NC - 2, NC - 1):
             in_block(c, l)
 

time: 207 us -> 199 us (0.961)
  Pallas kernels: 207 us -> 198 us
    pallas_call x1, Pallas kernels: 205 us -> 196 us  [per_device(): pl.pallas_call(kernel, out_shape=[pltpu.VMEM(o.shape, o.dtype) for o in o...]
where the time goes in v4:
time: 199 us; the launch traced here: 198 us
  Pallas kernels  198 us (99%)
    pallas_call x1, Pallas kernels, per_device(): pl.pallas_call(kernel, out_shape=[pltpu.VMEM(o.shape, o.dtype) for o in o...  196 us

profile of v4, /device:TPU:1, one launch (start us, length us, event | category | flops | bytes accessed | tf_op | source)
XLA Modules:
  0.0 198.4 jit_solution(13939646116386919157)
XLA Ops:
  0.6 196.0 %monarch.1 = (bf16[1024,512]{1,0:T(8,128)(2,1)S(1)}, bf16[1024,512]{1,0:T(8,128)(2,1)S(1)}, f32[4,16,512]{2,1,0:T(8,128)S(1)}, f32[4,64,512]{2,1,0:T(8,128)S(1)}...) custom-call(bf16[1024,512]{1,0:T(8,128)(2,1)} %tok_h.1, bf16[4,128,512]{2,1,0:T(8,128)(2,1)} %w1_h.1, ...), custom_call_target="tpu_custom_call" | custom-call | flops 16106127360 | bytes 11534336 | tf_op jit(solution)/shard_map/monarch/pallas_call | solution.py:545
  196.7 1.8 hand_over.1

commit v5 on v4

--- a/solution.py
+++ b/solution.py
@@ -68,7 +68,7 @@
         pltpu.make_async_copy(a, b, ld.at[i])
         for i, (a, b) in enumerate(((dl_h, dl), (og_h, og), (w1_h, w1), (tok_h, tok), (ul_h, ul), (df_h, df)))
     ]
-    for load in loads:
+    for load in loads[:4]:
         load.start()
 
     barrier = pltpu.get_barrier_semaphore()
@@ -172,26 +172,22 @@
             send_a[c, 8 * g:8 * g + 8] = tiles(parts, 8)
         send(0, c, send_a, recv_a)
 
-    def to_eight(ph, c, sbuf, rbuf, mate, place, target):
-        def one(i, _):
-            k = lax.rem(place + i, 8)
+    def to_eight(ph, c, sbuf, rbuf, mate, ways):
+        def one(i):
+            k, device = ways[i]
             for half, src in ((0, me), (8, mate)):
                 remote(
-                    sbuf.at[c, half + k], rbuf.at[c, src], ssem.at[ph, c], rsem.at[ph, c], tensor=target(k)
+                    sbuf.at[c, half + k], rbuf.at[c, src], ssem.at[ph, c], rsem.at[ph, c], tensor=device
                 ).start()
-            return 0
 
         for half, src in ((0, me), (8, mate)):
-            pltpu.make_async_copy(sbuf.at[c, half + place], rbuf.at[c, src], rsem.at[ph, c]).start()
+            pltpu.make_async_copy(sbuf.at[c, half + ways[0][0]], rbuf.at[c, src], rsem.at[ph, c]).start()
         return one
 
     def together(*ops):
-        def one(i, _):
+        for i in range(1, 8):
             for op in ops:
-                op(i, 0)
-            return 0
-
-        lax.fori_loop(1, 8, one, 0)
+                op(i)
 
     def first_stage(c, _):
         parts = [mm_nt(w1t[l, :, mz].reshape(256, D), tok[rows(c), D * l:D * l + D]) for l in range(NB)]
@@ -202,7 +198,11 @@
         return 0
 
     def first_send(c):
-        return to_eight(0, c, send_a, recv_a, mate_z, 2 * mx + mc, lambda k: 4 * (k // 2) + 2 * mz + lax.rem(k, 2))
+        ways = []
+        for dx, dc in ((0, 0), (1, 0), (3, 0), (2, 0), (1, 1), (3, 1), (2, 1), (0, 1)):
+            px, pc = lax.rem(mx + dx, 4), lax.rem(mc + dc, 2)
+            ways.append((2 * px + pc, 4 * px + 2 * mz + pc))
+        return to_eight(0, c, send_a, recv_a, mate_z, ways)
 
     def gmd_stage(c, _):
         s = lax.rem(c, 2)
@@ -216,11 +216,15 @@
         return 0
 
     def gmd_send(c):
-        s = lax.rem(c, 2)
-        return to_eight(
-            2, c, send_c, recv_c, mate_x(s), 4 * own_place(s) + zc,
-            lambda k: 4 * own_x(s, k // 4) + lax.rem(k, 4),
-        )
+        s = c % 2
+        ways = []
+        for dh, dz, dc in (
+            (0, 0, 0), (1, 0, 0), (0, 1, 0), (1, 1, 0), (0, 1, 1), (1, 0, 1), (1, 1, 1), (0, 0, 1)
+        ):
+            ph = lax.rem(own_place(s) + dh, 2)
+            pzc = 2 * lax.rem(mz + dz, 2) + lax.rem(mc + dc, 2)
+            ways.append((4 * ph + pzc, 4 * own_x(s, ph) + pzc))
+        return to_eight(2, c, send_c, recv_c, mate_x(s), ways)
 
     def mid_stage(c, _):
         wait_recv(0, c, recv_a)
@@ -360,6 +364,8 @@
     loads[3].wait()
     tok_copy(1).start()
     first_plain(0)
+    loads[4].start()
+    loads[5].start()
     pass_on(0, pdl.at[0])
     pass_on(1, pdl.at[1])
     pass_on(2, pw1)
@@ -382,11 +388,11 @@
     passed(1, pdl.at[1])
     lax.fori_loop(0, 2, gmd_stage, 0)
     passed(2, pw1)
-    first_stage(1, 0)
-    together(gmd_send(0), gmd_send(1), first_send(1))
+    lax.fori_loop(1, 3, first_stage, 0)
+    together(gmd_send(0), gmd_send(1), first_send(1), first_send(2))
     lax.fori_loop(2, NC, gmd_stage, 0)
-    lax.fori_loop(2, NC, first_stage, 0)
-    together(gmd_send(2), gmd_send(3), first_send(2), first_send(3))
+    first_stage(3, 0)
+    together(gmd_send(2), gmd_send(3), first_send(3))
     loads[4].wait()
     loads[5].wait()
     lax.fori_loop(0, NB, prep, 0)
@@ -460,11 +466,13 @@
             arrived(recv_d.at[c, :, l], qd.at[c - NC + 2, l])
             acc = acc + ur_term(c, l)
         gurs[l] = acc.T.reshape(8, 16, H).astype(BF)
-        for k in range(1, 8):
+        for k in (6, 2, 5, 7, 3, 1, 4):
             ur_copy(l, k).start()
-    for l in range(NB):
-        for c in (NC - 2, NC - 1):
-            in_block(c, l)
+        if l < NB - 1:
+            for c in (NC - 2, NC - 1):
+                in_block(c, l)
+    for c in (NC - 2, NC - 1):
+        in_block(c, NB - 1)
 
     def drain(c, _):
         wait_send(1, c, send_a)

time: 199 us -> 198 us (level)
  no operation moved by 1% of the time
where the time goes in v5:
time: 198 us
  Pallas kernels  197 us (99%)
    pallas_call x1, Pallas kernels, per_device(): pl.pallas_call(kernel, out_shape=[pltpu.VMEM(o.shape, o.dtype) for o in o...  195 us

profile of v5, /device:TPU:1, one launch (start us, length us, event | category | flops | bytes accessed | tf_op | source)
XLA Modules:
  0.0 197.7 jit_solution(2755622678391944317)
XLA Ops:
  0.6 195.3 %monarch.1 = (bf16[1024,512]{1,0:T(8,128)(2,1)S(1)}, bf16[1024,512]{1,0:T(8,128)(2,1)S(1)}, f32[4,16,512]{2,1,0:T(8,128)S(1)}, f32[4,64,512]{2,1,0:T(8,128)S(1)}...) custom-call(bf16[1024,512]{1,0:T(8,128)(2,1)} %tok_h.1, bf16[4,128,512]{2,1,0:T(8,128)(2,1)} %w1_h.1, ...), custom_call_target="tpu_custom_call" | custom-call | flops 16106127360 | bytes 11534336 | tf_op jit(solution)/shard_map/monarch/pallas_call | solution.py:553
  195.9 1.8 hand_over.1

commit v6 on v5

--- a/solution.py
+++ b/solution.py
@@ -426,7 +426,11 @@
     ulx = (1, ult, r1_ul, p2s_ul, p2r_ul, gul_o)
     scatter_y(*ulx[:3])
 
-    lax.fori_loop(0, NC, out_stage, 0)
+    lax.fori_loop(0, 2, out_stage, 0)
+    add_y(*dr)
+    out_stage(2, 0)
+    add_y(*ulx)
+    out_stage(3, 0)
 
     for j in range(NB):
         for g in range(2):
@@ -438,8 +442,6 @@
     dlx = (2, gdls, r1_dl, p2s_dl, p2r_dl, gdl_o)
     scatter_y(*dlx[:3])
 
-    add_y(*dr)
-    add_y(*ulx)
     add_y(*dlx)
 
     def in_wait(c, _):

time: 198 us -> 198 us (level)
  no operation moved by 1% of the time
where the time goes in v6:
time: 198 us
  Pallas kernels  197 us (99%)
    pallas_call x1, Pallas kernels, per_device(): pl.pallas_call(kernel, out_shape=[pltpu.VMEM(o.shape, o.dtype) for o in o...  195 us

profile of v6, /device:TPU:1, one launch (start us, length us, event | category | flops | bytes accessed | tf_op | source)
XLA Modules:
  0.0 197.7 jit_solution(17835221180042443037)
XLA Ops:
  0.6 195.3 %monarch.1 = (bf16[1024,512]{1,0:T(8,128)(2,1)S(1)}, bf16[1024,512]{1,0:T(8,128)(2,1)S(1)}, f32[4,16,512]{2,1,0:T(8,128)S(1)}, f32[4,64,512]{2,1,0:T(8,128)S(1)}...) custom-call(bf16[1024,512]{1,0:T(8,128)(2,1)} %tok_h.1, bf16[4,128,512]{2,1,0:T(8,128)(2,1)} %w1_h.1, ...), custom_call_target="tpu_custom_call" | custom-call | flops 16106127360 | bytes 11534336 | tf_op jit(solution)/shard_map/monarch/pallas_call | solution.py:555
  195.9 1.8 hand_over.1
